TPU v7x, 128 devices: a whole 4x4x4 slice. The times are simulated.
128 devices in a mesh: dp: 8 (over x_lo, z), tensor: 16 (over x_hi, y, core).
Axes of the slice: x: 4 (x_hi: 2, x_lo: 2; x = x_hi * 2 + x_lo), y: 4, z: 4, core: 2. Of those that a mesh axis runs over, the one named last changes fastest.
Arguments:
- tokens: bfloat16 [8, 2048, 4096], P('dp', 'tensor'), may hold values from -1.8 to 1.8
- cotangent: bfloat16 [8, 2048, 4096], P('dp', None, 'tensor'), may hold values from -6 to 6
- gain: float32 [4096], replicated, may hold values from 0.25 to 3.5
- w_query: bfloat16 [4096, 4096], P(None, 'tensor'), may hold values from -6 to 6
- w_key: bfloat16 [4096, 512], P(None, 'tensor'), may hold values from -6 to 6
- w_value: bfloat16 [4096, 512], P(None, 'tensor'), may hold values from -6 to 6
- moment_query: float32 [4096, 4096], P('dp', 'tensor'), may hold values from -6 to 6
- moment_key: float32 [4096, 512], P('dp', 'tensor'), may hold values from -6 to 6
- moment_value: float32 [4096, 512], P('dp', 'tensor'), may hold values from -6 to 6
Outputs:
- attended: bfloat16 [8, 2048, 4096], P('dp', None, 'tensor')
- grad_tokens: bfloat16 [8, 2048, 4096], P('dp', 'tensor')
- fresh_query: bfloat16 [4096, 4096], P(None, 'tensor')
- fresh_key: bfloat16 [4096, 512], P(None, 'tensor')
- fresh_value: bfloat16 [4096, 512], P(None, 'tensor')
- next_query: float32 [4096, 4096], P('dp', 'tensor')
- next_key: float32 [4096, 512], P('dp', 'tensor')
- next_value: float32 [4096, 512], P('dp', 'tensor')
All inputs are finite; a program needn't handle non-finite values.
Results may differ from a plain program's by a relative error of at most 0.017.
Values may be sent and summed in bfloat16 or wider, within the bound.
A program may use at most 256 MiB of HBM per device.

v0:
```python
import jax
import jax.numpy as jnp
from jax import lax
from jax.sharding import Mesh
from jax.sharding import PartitionSpec as P

D = 4096
HEADS = 32
KVH = 4
HD = 128
TENSOR = ("tensor_0", "tensor_1", "tensor_2")
DP = ("dp_0", "dp_1")
DP_TENSOR = ("dp_0", "dp_1", "tensor_0", "tensor_1", "tensor_2")
rope_base = 1000000.0
norm_eps = 1e-06
stat_eps = 1e-06
learn_rate = 0.05
keep_rate = 0.9


def partner_2(shard, axis, distance):
    return lax.ppermute(shard, axis, [(i, i ^ 1 << distance) for i in range(lax.axis_size(axis))])


def in_blocks(shard, dim, size):
    lengths = shard.shape
    pieces = shard.reshape(*lengths[:dim], size, lengths[dim] // size, *lengths[dim + 1 :])
    return jnp.moveaxis(pieces, dim, 0)


def summed_rows(shard, chips, core, dim):
    sizes = (lax.axis_size(chips), lax.axis_size(core))
    pieces = in_blocks(shard, dim, sizes[0] * sizes[1])
    inside = pieces.shape[1:]
    pieces = pieces.reshape(*sizes, *inside).swapaxes(0, 1).reshape(-1, *inside)
    pieces = lax.psum_scatter(pieces, core, scatter_dimension=0, tiled=True)
    return lax.psum_scatter(pieces, chips, scatter_dimension=0, tiled=True)[0]


def side_by_side(arrays, axis, dim, along):
    both = jnp.concatenate(arrays, axis=along)
    out, at, done = (lax.psum_scatter(both, axis, scatter_dimension=dim, tiled=True), 0, [])
    for a in arrays:
        done.append(lax.slice_in_dim(out, at, at + a.shape[along], axis=along))
        at += a.shape[along]
    return tuple(done)


def one_axis_at_a_time(shard, axes):
    for axis in axes:
        shard = lax.psum(shard, axis)
    return shard


def in_one_piece(arrays, axis, dim, along):
    ends, at = ([], 0)
    for a in arrays[:-1]:
        at += a.shape[along]
        ends.append(at)
    both = jnp.concatenate(arrays, axis=along)
    return tuple(jnp.split(lax.all_gather(both, axis, axis=dim, tiled=True), ends, axis=along))


def rotate(matrix, first_column, head_size, sign):
    length = matrix.shape[0]
    columns = matrix.shape[1]
    index = first_column + jnp.arange(columns, dtype=jnp.int32)
    within = index % head_size // 2
    rates = jnp.power(jnp.float32(rope_base), within.astype(jnp.float32) * (-2.0 / head_size))
    angle = jnp.arange(length, dtype=jnp.float32)[:, None] * rates[None, :]
    even = index % 2 == 0
    partner = jnp.where(even[None, :], -jnp.roll(matrix, -1, axis=1), jnp.roll(matrix, 1, axis=1))
    return matrix * jnp.cos(angle) + partner * (sign * jnp.sin(angle))


def per_device(
    tokens, cotangent, gain, w_query, w_key, w_value, moment_query, moment_key, moment_value
):
    rank = lax.axis_index(TENSOR)
    query_width = w_query.shape[1]
    key_width = w_key.shape[1]
    local_heads = query_width // HD
    width = tokens.shape[2]
    in_scale = width ** (-0.5)
    head_scale = HD ** (-0.5)
    inputs = tokens[0].astype(jnp.float32)
    reciprocal = lax.rsqrt(jnp.mean(inputs * inputs, axis=1, keepdims=True) + norm_eps)
    unit_rows = inputs * reciprocal
    normed = (unit_rows * gain).astype(jnp.bfloat16)
    normed_all = lax.all_gather(normed, TENSOR, axis=0, tiled=True)
    length = normed_all.shape[0]
    query = rotate(
        jnp.dot(normed_all, w_query, preferred_element_type=jnp.float32) * in_scale,
        rank * query_width,
        HD,
        1.0,
    ).astype(jnp.bfloat16)
    key_part = rotate(
        jnp.dot(normed_all, w_key, preferred_element_type=jnp.float32) * in_scale,
        rank * key_width,
        HD,
        1.0,
    ).astype(jnp.bfloat16)
    value_part = (
        jnp.dot(normed_all, w_value, preferred_element_type=jnp.float32) * in_scale
    ).astype(jnp.bfloat16)
    span = lax.axis_size(TENSOR) // KVH
    levels = span.bit_length() - 1
    paired = jnp.stack([key_part, value_part])
    for level in range(levels):
        other = partner_2(paired, TENSOR, level)
        higher = rank // 2**level % 2 == 1
        paired = jnp.where(
            higher,
            jnp.concatenate([other, paired], axis=2),
            jnp.concatenate([paired, other], axis=2),
        )
    key_head = paired[0]
    value_head = paired[1]
    query_heads = query.reshape(length, local_heads, HD)
    grad_heads = cotangent[0].reshape(length, local_heads, HD)
    rows_block = 512
    starts = jnp.arange(length // rows_block, dtype=jnp.int32) * rows_block
    places = jnp.arange(length)

    def attend(carry, start):
        query_rows = lax.dynamic_slice_in_dim(query_heads, start, rows_block, 0)
        grad_rows = lax.dynamic_slice_in_dim(grad_heads, start, rows_block, 0)
        scores = (
            jnp.einsum("shd,td->hst", query_rows, key_head, preferred_element_type=jnp.float32)
            * head_scale
        )
        row_places = start + jnp.arange(rows_block)
        causal = row_places[:, None] >= places[None, :]
        attention = jax.nn.softmax(jnp.where(causal[None], scores, -1e30), axis=2)
        attention_low = attention.astype(jnp.bfloat16)
        attended_rows = jnp.einsum(
            "hst,td->shd", attention_low, value_head, preferred_element_type=jnp.float32
        ).astype(jnp.bfloat16)
        grad_raw = jnp.einsum(
            "shd,td->hst", grad_rows, value_head, preferred_element_type=jnp.float32
        )
        grad_scores = attention * (grad_raw - jnp.sum(attention * grad_raw, axis=2, keepdims=True))
        grad_low = (grad_scores * head_scale).astype(jnp.bfloat16)
        query_grad_rows = jnp.einsum(
            "hst,td->shd", grad_low, key_head, preferred_element_type=jnp.float32
        )
        key_term = jnp.einsum(
            "hst,shd->td", grad_low, query_rows, preferred_element_type=jnp.float32
        )
        value_term = jnp.einsum(
            "hst,shd->td", attention_low, grad_rows, preferred_element_type=jnp.float32
        )
        return ((carry[0] + key_term, carry[1] + value_term), (attended_rows, query_grad_rows))

    empty = jnp.zeros((length, HD), jnp.float32)
    (key_local, value_local), (attended_blocks, query_blocks) = lax.scan(
        attend, (empty, empty), starts
    )
    attended = attended_blocks.reshape(length, query_width)
    grad_query_raw = query_blocks.reshape(length, query_width)
    current = lax.optimization_barrier(
        jnp.stack([key_local, value_local]).astype(jnp.bfloat16)
    ).astype(jnp.float32)
    for level in reversed(range(levels)):
        middle = current.shape[2] // 2
        higher = rank // 2**level % 2 == 1
        outgoing = jnp.where(higher, current[:, :, :middle], current[:, :, middle:])
        retained = jnp.where(higher, current[:, :, middle:], current[:, :, :middle])
        current = retained + partner_2(outgoing.astype(jnp.bfloat16), TENSOR, level).astype(
            outgoing.dtype
        )
    grad_key = rotate(current[0], rank * key_width, HD, -1.0).astype(jnp.bfloat16)
    grad_value = current[1].astype(jnp.bfloat16)
    grad_query = rotate(grad_query_raw, rank * query_width, HD, -1.0).astype(jnp.bfloat16)

    def product(grad, weight):
        return jnp.einsum("sc,dc->sd", grad, weight, preferred_element_type=jnp.float32)

    grad_normed = summed_rows(
        (
            (product(grad_query, w_query) + product(grad_key, w_key) + product(grad_value, w_value))
            * in_scale
        ).astype(jnp.bfloat16),
        ("tensor_0", "tensor_1"),
        "tensor_2",
        0,
    ).astype(jnp.float32)
    grad_unit = grad_normed * gain
    inner = jnp.mean(grad_unit * unit_rows, axis=1, keepdims=True)
    grad_tokens = (reciprocal * (grad_unit - unit_rows * inner)).astype(jnp.bfloat16)[None]
    grad_wq = (
        jnp.einsum("sd,sc->dc", normed_all, grad_query, preferred_element_type=jnp.float32)
        * in_scale
    )
    grad_wk = (
        jnp.einsum("sd,sc->dc", normed_all, grad_key, preferred_element_type=jnp.float32) * in_scale
    )
    grad_wv = (
        jnp.einsum("sd,sc->dc", normed_all, grad_value, preferred_element_type=jnp.float32)
        * in_scale
    )
    summed_query, summed_key, summed_value = tuple(
        (
            part.astype(jnp.float32)
            for part in side_by_side(
                (
                    grad_wq.astype(jnp.bfloat16),
                    grad_wk.astype(jnp.bfloat16),
                    grad_wv.astype(jnp.bfloat16),
                ),
                DP,
                0,
                1,
            )
        )
    )
    square = (
        jnp.sum(summed_query * summed_query)
        + jnp.sum(summed_key * summed_key)
        + jnp.sum(summed_value * summed_value)
    )
    total = one_axis_at_a_time(square, DP_TENSOR)
    count_all = 1.0 * D * HD * (HEADS + 2 * KVH)
    factor = lax.rsqrt(total / count_all + stat_eps)
    dp_rank = lax.axis_index(DP)

    def advance(weight_own, moment, summed):
        moved = keep_rate * moment + summed * factor
        return ((weight_own.astype(jnp.float32) - learn_rate * moved).astype(jnp.bfloat16), moved)

    share = moment_query.shape[0]
    own_query = lax.dynamic_slice_in_dim(w_query, dp_rank * share, share, 0)
    own_key = lax.dynamic_slice_in_dim(w_key, dp_rank * share, share, 0)
    own_value = lax.dynamic_slice_in_dim(w_value, dp_rank * share, share, 0)
    part_query, next_query = advance(own_query, moment_query, summed_query)
    part_key, next_key = advance(own_key, moment_key, summed_key)
    part_value, next_value = advance(own_value, moment_value, summed_value)
    fresh_query, fresh_key, fresh_value = in_one_piece((part_query, part_key, part_value), DP, 0, 1)
    return (
        attended[None],
        grad_tokens,
        fresh_query,
        fresh_key,
        fresh_value,
        next_query,
        next_key,
        next_value,
    )


def solution(mesh):
    torus = Mesh(
        mesh.devices.reshape(2, 4, 2, 4, 2), ("dp_0", "dp_1", "tensor_0", "tensor_1", "tensor_2")
    )
    placed = (
        P(DP, TENSOR, None),
        P(DP, None, TENSOR),
        P(),
        P(None, TENSOR),
        P(None, TENSOR),
        P(None, TENSOR),
        P(DP, TENSOR),
        P(DP, TENSOR),
        P(DP, TENSOR),
    )
    return jax.shard_map(
        per_device,
        mesh=torus,
        in_specs=placed,
        out_specs=(
            P(DP, None, TENSOR),
            P(DP, TENSOR, None),
            P(None, TENSOR),
            P(None, TENSOR),
            P(None, TENSOR),
            P(DP, TENSOR),
            P(DP, TENSOR),
            P(DP, TENSOR),
        ),
        check_vma=False,
    )
```

profile of v0, /device:TPU:1, one launch (start us, length us, event | category | flops | bytes accessed | tf_op | source)
XLA Modules:
  0.0 772.4 jit_solution(11540395952958526187)
XLA Ops:
  13.9 111.1 %all-gather.3.cloned.1.call-done = bf16[2048,4096]{1,0:T(8,128)(2,1)} async-done(((bf16[128,4096]{1,0:T(8,128)(2,1)}), bf16[2048,4096]{1,0:T(8,128)(2,1)}) %all-gather.3.cloned.1.call-update) | async-done | bytes 16777232 | tf_op jit(solution)/shard_map/all_gather | solution.py:90
  125.0 10.9 %convolution_multiply_fusion.5 = f32[2048,32]{0,1:T(8,128)S(1)} fusion(bf16[2048,4096]{1,0:T(8,128)(2,1)} %all-gather.3.cloned.1.call-done, bf16[4096,32]{0,1:T(8,128)(2,1)S(1)} %copy-done.11), kind=kOutput, calls=%fused_computation.75 | convolution fusion | flops 536936448 | bytes 17301504 | tf_op jit(solution)/shard_map/dot_general | solution.py:99
  143.0 9.7 %convolution_multiply_fusion.3 = f32[2048,256]{0,1:T(8,128)} fusion(bf16[2048,4096]{1,0:T(8,128)(2,1)} %all-gather.3.cloned.1.call-done, bf16[4096,256]{1,0:T(8,128)(2,1)S(1)} %copy-done), kind=kOutput, calls=%fused_computation.64 | convolution fusion | flops 4295491584 | bytes 20971520 | tf_op jit(solution)/shard_map/dot_general | solution.py:93
  155.9 10.3 %fusion.83 = bf16[2048,256]{0,1:T(8,128)(2,1)} fusion(f32[2048,1]{0,1:T(1,128)S(1)} %get-tuple-element.180, f32[2048,255]{0,1:T(8,128)S(1)} %get-tuple-element.182, f32[2048,255]{0,1:T(8,128)S(1)} %get-tuple-element.181, f32[2048,1]{0,1:T(1,128)S(1)} %get-tuple-element.179, f32[2048,256]{0,1:T(8,128)S(1)} %copy-done.4, f32[256]{0:T(256)S(1)} %multiply_power_fusion, ...), kind=kLoop, calls=%fused_computation.90 | loop fusion | flops 4718592 | bytes 7341312 | tf_op jit(solution)/shard_map/convert_element_type | solution.py:97
  171.4 280.0 %while.17 = (s32[]{:T(128)}, f32[2048,128]{1,0:T(8,128)}, f32[2048,128]{1,0:T(8,128)}, bf16[4,512,2,128]{3,2,1,0:T(2,128)(2,1)}, f32[4,512,2,128]{1,0,3,2:T(4,12...) while((s32[]{:T(128)}, f32[2048,128]{1,0:T(8,128)}, ...), condition=%wide.region_5.6_spmd.clone, body=%wide.region_1.5_spmd.clone.sunk | while | flops 3269599744 | bytes 147091824 | solution.py:157
  175.3 8.0 %fusion.179 = (f32[2,512]{1,0:T(2,128)S(1)}, f32[2,512,2048]{2,1,0:T(8,128)}) fusion(pred[512,2048]{1,0:T(8,128)(4,1)S(1)} %iota_compare_fusion.2, bf16[2048,128]{1,0:T(8,128)(2,1)} %get-tuple-element.293, bf16[2048,2,128]{0,2,1:T(8,128)(2,1)} %get-tuple-element.292, s32[]{:T(128)S(6)} %select_n.260), kind=kOutput, calls=%fused_computation.174.clone.1 | convolution fusion | flops 545261568 | bytes 10227716 | tf_op jit(solution)/shard_map/while/body/eval_jaxpr/sub | solution.py:135
  197.7 12.8 %fusion.183 = f32[1,512,2,128]{3,1,2,0:T(8,128)S(1)} fusion(f32[512,2,2048]{2,0,1:T(8,128)} %fusion.178, bf16[2048,128]{1,0:T(8,128)(2,1)S(1)} %copy-done.18, f32[2,512,2048]{2,1,0:T(8,128)} %get-tuple-element.258, f32[2,512]{1,0:T(2,128)S(1)} %get-tuple-element.259), kind=kOutput, calls=%fused_computation.28.clone.1 | convolution fusion | flops 551554048 | bytes 17829888 | tf_op jit(solution)/shard_map/while/body/eval_jaxpr/hst,td->shd/dot_general | solution.py:145
  210.5 19.4 %fusion.180 = f32[2048,128]{1,0:T(8,128)} fusion(f32[512,2,2048]{2,0,1:T(8,128)} %fusion.178, f32[2048,128]{1,0:T(8,128)} %get-tuple-element.274, pred[]{:T(512)S(6)} %compare.38, bf16[2048,2,128]{0,2,1:T(8,128)(2,1)} %get-tuple-element.292, s32[]{:T(128)S(6)} %select_n.260, f32[2,512,2048]{2,1,0:T(8,128)} %get-tuple-element.258, ...), kind=kOutput, calls=%fused_computation.24.clone.1 | convolution fusion | flops 552078336 | bytes 35921924 | tf_op jit(solution)/shard_map/while/body/eval_jaxpr/hst,shd->td/dot_general | solution.py:148
  230.3 11.1 %dynamic_update_slice.14 = f32[4,512,2,128]{1,0,3,2:T(4,128)} dynamic-update-slice(f32[4,512,2,128]{1,0,3,2:T(4,128)} %get-tuple-element.277, f32[1,512,2,128]{1,0,3,2:T(1,128)S(1)} %copy.66, s32[]{:T(128)S(6)} %copy.74, s32[]{:T(128)} %constant.177.clone.1..sunk, s32[]{:T(128)} %constant.177.clone.1..sunk, s32[]{:T(128)} %constant.177.clone.1..sunk) | dynamic-update-slice | bytes 1048580 | tf_op jit(solution)/shard_map/while/body/jit(dynamic_update_index_in_dim)/dynamic_update_slice | solution.py:157
  245.2 8.0 %fusion.179 = (f32[2,512]{1,0:T(2,128)S(1)}, f32[2,512,2048]{2,1,0:T(8,128)}) fusion(pred[512,2048]{1,0:T(8,128)(4,1)S(1)} %iota_compare_fusion.2, bf16[2048,128]{1,0:T(8,128)(2,1)} %get-tuple-element.293, bf16[2048,2,128]{0,2,1:T(8,128)(2,1)} %get-tuple-element.292, s32[]{:T(128)S(6)} %select_n.260), kind=kOutput, calls=%fused_computation.174.clone.1 | convolution fusion | flops 545261568 | bytes 10227716 | tf_op jit(solution)/shard_map/while/body/eval_jaxpr/sub | solution.py:135
  267.6 12.8 %fusion.183 = f32[1,512,2,128]{3,1,2,0:T(8,128)S(1)} fusion(f32[512,2,2048]{2,0,1:T(8,128)} %fusion.178, bf16[2048,128]{1,0:T(8,128)(2,1)S(1)} %copy-done.18, f32[2,512,2048]{2,1,0:T(8,128)} %get-tuple-element.258, f32[2,512]{1,0:T(2,128)S(1)} %get-tuple-element.259), kind=kOutput, calls=%fused_computation.28.clone.1 | convolution fusion | flops 551554048 | bytes 17829888 | tf_op jit(solution)/shard_map/while/body/eval_jaxpr/hst,td->shd/dot_general | solution.py:145
  280.4 19.4 %fusion.180 = f32[2048,128]{1,0:T(8,128)} fusion(f32[512,2,2048]{2,0,1:T(8,128)} %fusion.178, f32[2048,128]{1,0:T(8,128)} %get-tuple-element.274, pred[]{:T(512)S(6)} %compare.38, bf16[2048,2,128]{0,2,1:T(8,128)(2,1)} %get-tuple-element.292, s32[]{:T(128)S(6)} %select_n.260, f32[2,512,2048]{2,1,0:T(8,128)} %get-tuple-element.258, ...), kind=kOutput, calls=%fused_computation.24.clone.1 | convolution fusion | flops 552078336 | bytes 35921924 | tf_op jit(solution)/shard_map/while/body/eval_jaxpr/hst,shd->td/dot_general | solution.py:148
  300.2 11.1 %dynamic_update_slice.14 = f32[4,512,2,128]{1,0,3,2:T(4,128)} dynamic-update-slice(f32[4,512,2,128]{1,0,3,2:T(4,128)} %get-tuple-element.277, f32[1,512,2,128]{1,0,3,2:T(1,128)S(1)} %copy.66, s32[]{:T(128)S(6)} %copy.74, s32[]{:T(128)} %constant.177.clone.1..sunk, s32[]{:T(128)} %constant.177.clone.1..sunk, s32[]{:T(128)} %constant.177.clone.1..sunk) | dynamic-update-slice | bytes 1048580 | tf_op jit(solution)/shard_map/while/body/jit(dynamic_update_index_in_dim)/dynamic_update_slice | solution.py:157
  315.1 8.0 %fusion.179 = (f32[2,512]{1,0:T(2,128)S(1)}, f32[2,512,2048]{2,1,0:T(8,128)}) fusion(pred[512,2048]{1,0:T(8,128)(4,1)S(1)} %iota_compare_fusion.2, bf16[2048,128]{1,0:T(8,128)(2,1)} %get-tuple-element.293, bf16[2048,2,128]{0,2,1:T(8,128)(2,1)} %get-tuple-element.292, s32[]{:T(128)S(6)} %select_n.260), kind=kOutput, calls=%fused_computation.174.clone.1 | convolution fusion | flops 545261568 | bytes 10227716 | tf_op jit(solution)/shard_map/while/body/eval_jaxpr/sub | solution.py:135
  337.5 12.8 %fusion.183 = f32[1,512,2,128]{3,1,2,0:T(8,128)S(1)} fusion(f32[512,2,2048]{2,0,1:T(8,128)} %fusion.178, bf16[2048,128]{1,0:T(8,128)(2,1)S(1)} %copy-done.18, f32[2,512,2048]{2,1,0:T(8,128)} %get-tuple-element.258, f32[2,512]{1,0:T(2,128)S(1)} %get-tuple-element.259), kind=kOutput, calls=%fused_computation.28.clone.1 | convolution fusion | flops 551554048 | bytes 17829888 | tf_op jit(solution)/shard_map/while/body/eval_jaxpr/hst,td->shd/dot_general | solution.py:145
  350.3 19.4 %fusion.180 = f32[2048,128]{1,0:T(8,128)} fusion(f32[512,2,2048]{2,0,1:T(8,128)} %fusion.178, f32[2048,128]{1,0:T(8,128)} %get-tuple-element.274, pred[]{:T(512)S(6)} %compare.38, bf16[2048,2,128]{0,2,1:T(8,128)(2,1)} %get-tuple-element.292, s32[]{:T(128)S(6)} %select_n.260, f32[2,512,2048]{2,1,0:T(8,128)} %get-tuple-element.258, ...), kind=kOutput, calls=%fused_computation.24.clone.1 | convolution fusion | flops 552078336 | bytes 35921924 | tf_op jit(solution)/shard_map/while/body/eval_jaxpr/hst,shd->td/dot_general | solution.py:148
  370.1 11.1 %dynamic_update_slice.14 = f32[4,512,2,128]{1,0,3,2:T(4,128)} dynamic-update-slice(f32[4,512,2,128]{1,0,3,2:T(4,128)} %get-tuple-element.277, f32[1,512,2,128]{1,0,3,2:T(1,128)S(1)} %copy.66, s32[]{:T(128)S(6)} %copy.74, s32[]{:T(128)} %constant.177.clone.1..sunk, s32[]{:T(128)} %constant.177.clone.1..sunk, s32[]{:T(128)} %constant.177.clone.1..sunk) | dynamic-update-slice | bytes 1048580 | tf_op jit(solution)/shard_map/while/body/jit(dynamic_update_index_in_dim)/dynamic_update_slice | solution.py:157
  385.1 8.0 %fusion.179 = (f32[2,512]{1,0:T(2,128)S(1)}, f32[2,512,2048]{2,1,0:T(8,128)}) fusion(pred[512,2048]{1,0:T(8,128)(4,1)S(1)} %iota_compare_fusion.2, bf16[2048,128]{1,0:T(8,128)(2,1)} %get-tuple-element.293, bf16[2048,2,128]{0,2,1:T(8,128)(2,1)} %get-tuple-element.292, s32[]{:T(128)S(6)} %select_n.260), kind=kOutput, calls=%fused_computation.174.clone.1 | convolution fusion | flops 545261568 | bytes 10227716 | tf_op jit(solution)/shard_map/while/body/eval_jaxpr/sub | solution.py:135
  407.4 12.8 %fusion.183 = f32[1,512,2,128]{3,1,2,0:T(8,128)S(1)} fusion(f32[512,2,2048]{2,0,1:T(8,128)} %fusion.178, bf16[2048,128]{1,0:T(8,128)(2,1)S(1)} %copy-done.18, f32[2,512,2048]{2,1,0:T(8,128)} %get-tuple-element.258, f32[2,512]{1,0:T(2,128)S(1)} %get-tuple-element.259), kind=kOutput, calls=%fused_computation.28.clone.1 | convolution fusion | flops 551554048 | bytes 17829888 | tf_op jit(solution)/shard_map/while/body/eval_jaxpr/hst,td->shd/dot_general | solution.py:145
  420.2 19.4 %fusion.180 = f32[2048,128]{1,0:T(8,128)} fusion(f32[512,2,2048]{2,0,1:T(8,128)} %fusion.178, f32[2048,128]{1,0:T(8,128)} %get-tuple-element.274, pred[]{:T(512)S(6)} %compare.38, bf16[2048,2,128]{0,2,1:T(8,128)(2,1)} %get-tuple-element.292, s32[]{:T(128)S(6)} %select_n.260, f32[2,512,2048]{2,1,0:T(8,128)} %get-tuple-element.258, ...), kind=kOutput, calls=%fused_computation.24.clone.1 | convolution fusion | flops 552078336 | bytes 35921924 | tf_op jit(solution)/shard_map/while/body/eval_jaxpr/hst,shd->td/dot_general | solution.py:148
  440.0 11.1 %dynamic_update_slice.14 = f32[4,512,2,128]{1,0,3,2:T(4,128)} dynamic-update-slice(f32[4,512,2,128]{1,0,3,2:T(4,128)} %get-tuple-element.277, f32[1,512,2,128]{1,0,3,2:T(1,128)S(1)} %copy.66, s32[]{:T(128)S(6)} %copy.74, s32[]{:T(128)} %constant.177.clone.1..sunk, s32[]{:T(128)} %constant.177.clone.1..sunk, s32[]{:T(128)} %constant.177.clone.1..sunk) | dynamic-update-slice | bytes 1048580 | tf_op jit(solution)/shard_map/while/body/jit(dynamic_update_index_in_dim)/dynamic_update_slice | solution.py:157
  460.4 11.9 %fusion.87 = bf16[2048,256]{0,1:T(8,128)(2,1)S(1)} fusion(f32[2048,1]{0,1:T(1,128)S(1)} %get-tuple-element.176, f32[2048,255]{0,1:T(8,128)} %get-tuple-element.178, f32[2048,255]{0,1:T(8,128)} %get-tuple-element.177, f32[2048,1]{0,1:T(1,128)S(1)} %get-tuple-element.175, f32[2048,256]{0,1:T(8,128)} %bitcast.183, f32[256]{0:T(256)S(1)} %copy-done.25, ...), kind=kLoop, calls=%fused_computation.95 | loop fusion | flops 5242880 | bytes 7341312 | tf_op jit(solution)/shard_map/convert_element_type | solution.py:175
  490.2 13.5 %fusion.135 = f32[2048,4096]{1,0:T(8,128)} fusion(bf16[2048,32]{0,1:T(8,128)(2,1)S(1)} %fusion.99, bf16[4096,32]{0,1:T(8,128)(2,1)S(1)} %copy-done.12), kind=kOutput, calls=%fused_computation.184 | convolution fusion | flops 536870912 | bytes 33947648 | tf_op jit(solution)/shard_map/sc,dc->sd/dot_general | solution.py:178
  503.8 13.3 %fusion.109 = f32[2048,4096]{1,0:T(8,128)} fusion(bf16[4096,32]{0,1:T(8,128)(2,1)S(1)} %copy-done.14, f32[2,2048,32]{1,2,0:T(8,128)S(1)} %convert_add_fusion.1), kind=kOutput, calls=%fused_computation.144 | convolution fusion | flops 536870912 | bytes 33947648 | tf_op jit(solution)/shard_map/sc,dc->sd/dot_general | solution.py:178
  517.1 28.8 %multiply_convert_fusion = bf16[2048,4096]{1,0:T(8,128)(2,1)} fusion(f32[2048,4096]{1,0:T(8,128)} %fusion.109, f32[2048,4096]{1,0:T(8,128)} %fusion.135, bf16[2048,256]{0,1:T(8,128)(2,1)} %copy-done.8, bf16[4096,256]{1,0:T(8,128)(2,1)S(1)} %copy-done), kind=kOutput, calls=%fused_computation.57 | convolution fusion | flops 4328521728 | bytes 87031808 | tf_op jit(solution)/shard_map/sc,dc->sd/dot_general | solution.py:178
  546.0 14.0 %copy.42 = bf16[2,8,128,4096]{3,2,1,0:T(8,128)(2,1)} copy(bf16[2,8,128,4096]{3,2,0,1:T(8,128)(2,1)} %bitcast.179) | data formatting | bytes 33554432 | tf_op jit(solution)/shard_map/transpose | solution.py:35
  569.5 9.4 %psum.36 = f32[]{:T(128)} all-reduce(f32[]{:T(128)} %psum.35), channel_id=1, replica_groups=mesh['dp_0'=2,'dp_1'=4,'tensor_0'=2,'tensor_1'=4,'tensor_2'=2] {'dp_1'}, use_global_device_ids=true, to_apply=%region_14.15 | all-reduce | flops 1 | bytes 8 | tf_op jit(solution)/shard_map/psum | solution.py:51
  578.9 5.9 psum.37
  585.7 7.2 psum.38
  594.2 9.2 %psum.39 = f32[]{:T(128)} all-reduce(f32[]{:T(128)} %psum.38), channel_id=1, replica_groups=mesh['dp_0'=2,'dp_1'=4,'tensor_0'=2,'tensor_1'=4,'tensor_2'=2] {'tensor_2'}, use_global_device_ids=true, to_apply=%region_17.18 | all-reduce | flops 1 | bytes 8 | tf_op jit(solution)/shard_map/psum | solution.py:51
  611.5 29.4 %all-gather.5.cloned.1.call-done = bf16[4096,320]{0,1:T(8,128)(2,1)} async-done(((bf16[512,320]{0,1:T(8,128)(2,1)}), bf16[4096,320]{0,1:T(8,128)(2,1)}) %all-gather.5.cloned.1.call-update) | async-done | bytes 2621456 | tf_op jit(solution)/shard_map/all_gather | solution.py:61
  650.1 112.2 %reduce-scatter.6.cloned.1.call-done = bf16[1,128,4096]{2,1,0:T(8,128)(2,1)} async-done(((bf16[8,128,4096]{2,1,0:T(8,128)(2,1)}), bf16[1,128,4096]{2,1,0:T(8,128)(2,1)}) %reduce-scatter.6.cloned.1.call-update) | async-done | bytes 1048592 | tf_op jit(solution)/shard_map/reduce_scatter | solution.py:37
  (215 shorter events, 144.7 us)
Async XLA Ops:
  7.2 135.9 %copy-start = (bf16[4096,256]{1,0:T(8,128)(2,1)S(1)}, bf16[4096,256]{1,0:T(8,128)(2,1)}, u32[]{:S(2)}) copy-start(bf16[4096,256]{1,0:T(8,128)(2,1)} %param.14) | copy-start | bytes 6291460
  7.2 117.8 %all-gather.3.cloned.1.call-start = ((), (), s32[]{:S(2)}) async-start(), calls=%async_computation.3 | async-start | bytes 17825792 | tf_op jit(solution)/shard_map/all_gather | solution.py:90
  9.5 115.5 %copy-start.11 = (bf16[4096,32]{0,1:T(8,128)(2,1)S(1)}, bf16[4096,32]{0,1:T(8,128)(2,1)}, u32[]{:S(2)}) copy-start(bf16[4096,32]{0,1:T(8,128)(2,1)} %param.15) | copy-start | bytes 786436
  12.1 547.9 %reduce-scatter.8.cloned.1.call-start = ((), (), s32[]{:S(2)}) async-start(), calls=%async_computation.6 | async-start | bytes 2949120 | tf_op jit(solution)/shard_map/reduce_scatter | solution.py:42
  13.8 122.3 %copy-start.26 = (pred[32]{0:T(512)(128)(4,1)}, pred[32]{0:T(512)(128)(4,1)S(1)}, u32[]{:S(2)}) copy-start(pred[32]{0:T(512)(128)(4,1)S(1)} %fusion.113) | copy-start | bytes 100
  13.8 122.3 %copy-start.28 = (f32[32]{0:T(128)}, f32[32]{0:T(128)S(1)}, u32[]{:S(2)}) copy-start(f32[32]{0:T(128)S(1)} %multiply_power_fusion.1) | copy-start | bytes 388
  13.8 142.0 %copy-start.30 = (pred[256]{0:T(512)(128)(4,1)}, pred[256]{0:T(512)(128)(4,1)S(1)}, u32[]{:S(2)}) copy-start(pred[256]{0:T(512)(128)(4,1)S(1)} %fusion.112) | copy-start | bytes 772
  13.9 142.0 %copy-start.24 = (f32[256]{0:T(256)}, f32[256]{0:T(256)S(1)}, u32[]{:S(2)}) copy-start(f32[256]{0:T(256)S(1)} %multiply_power_fusion) | copy-start | bytes 3076
  13.9 123.5 %copy-start.13 = (bf16[4096,32]{0,1:T(8,128)(2,1)S(1)}, bf16[4096,32]{0,1:T(8,128)(2,1)}, u32[]{:S(2)}) copy-start(bf16[4096,32]{0,1:T(8,128)(2,1)} %param.16) | copy-start | bytes 786436
  125.0 12.4 %copy-start.1 = (bf16[2048,4096]{1,0:T(8,128)(2,1)S(1)}, bf16[2048,4096]{1,0:T(8,128)(2,1)}, u32[]{:S(2)}) copy-start(bf16[2048,4096]{1,0:T(8,128)(2,1)} %all-gather.3.cloned.1.call-done) | copy-start | bytes 50331652
  142.5 13.1 %collective-permute-start = (bf16[2,2048,32]{1,2,0:T(8,128)(2,1)S(1)}, bf16[2,2048,32]{1,2,0:T(8,128)(2,1)S(1)}, u32[]{:S(2)}, u32[]{:S(2)}) collective-permute-start(bf16[2,2048,32]{1,2,0:T(8,128)(2,1)S(1)} %pad_maximum_fusion.3), channel_id=1, source_target_pairs={{0,1},{1,0},{2,3},{3,2},{4,5},{5,4},{6,7},{7,6},{8,9},{9,8},{10,11... | collective-permute-start | bytes 786440 | tf_op jit(solution)/shard_map/ppermute | solution.py:22
  155.8 13.3 %collective-permute-start.1 = (bf16[2,2048,64]{1,2,0:T(8,128)(2,1)S(1)}, bf16[2,2048,64]{1,2,0:T(8,128)(2,1)S(1)}, u32[]{:S(2)}, u32[]{:S(2)}) collective-permute-start(bf16[2,2048,64]{1,2,0:T(8,128)(2,1)S(1)} %maximum_select_fusion.1), channel_id=1, source_target_pairs={{0,2},{1,3},{2,0},{3,1},{4,6},{5,7},{6,4},{7,5},{8,10},{9,11},{10,... | collective-permute-start | bytes 1572872 | tf_op jit(solution)/shard_map/ppermute | solution.py:22
  183.3 5.9 copy-start.7
  183.3 5.9 copy-start.15
  183.3 6.7 copy-start.32
  253.2 6.7 copy-start.32
  323.1 6.7 copy-start.32
  393.1 6.7 copy-start.32
  459.6 15.2 %copy-start.2 = (bf16[2048,4096]{1,0:T(8,128)(2,1)S(1)}, bf16[2048,4096]{1,0:T(8,128)(2,1)}, u32[]{:S(2)}) copy-start(bf16[2048,4096]{1,0:T(8,128)(2,1)} %all-gather.3.cloned.1.call-done) | copy-start | bytes 50331652
  460.0 12.4 %collective-permute-start.2 = (bf16[2,2048,64]{1,2,0:T(8,128)(2,1)S(1)}, bf16[2,2048,64]{1,2,0:T(8,128)(2,1)S(1)}, u32[]{:S(2)}, u32[]{:S(2)}) collective-permute-start(bf16[2,2048,64]{1,2,0:T(8,128)(2,1)S(1)} %select_convert_fusion), channel_id=1, source_target_pairs={{0,2},{1,3},{2,0},{3,1},{4,6},{5,7},{6,4},{7,5},{8,10},{9,11},{10,... | collective-permute-start | bytes 1572872 | tf_op jit(solution)/shard_map/ppermute | solution.py:22
  472.3 7.1 copy-start.8
  472.7 6.8 collective-permute-start.3
  489.3 14.5 %copy-start.14 = (bf16[4096,32]{0,1:T(8,128)(2,1)S(1)}, bf16[4096,32]{0,1:T(8,128)(2,1)}, u32[]{:S(2)}) copy-start(bf16[4096,32]{0,1:T(8,128)(2,1)} %param.16) | copy-start | bytes 786436
  489.3 118.1 %reduce-scatter.4.cloned.1.call-start = ((), (), s32[]{:S(2)}) async-start(), calls=%async_computation.4 | async-start | bytes 25165824 | tf_op jit(solution)/shard_map/reduce_scatter | solution.py:36
  559.9 44.1 %copy-start.20 = (f32[512,32]{0,1:T(8,128)S(1)}, f32[512,32]{0,1:T(8,128)}, u32[]{:S(2)}) copy-start(f32[512,32]{0,1:T(8,128)} %param.18) | copy-start | bytes 196612
  560.0 44.1 %copy-start.21 = (f32[512,32]{0,1:T(8,128)S(1)}, f32[512,32]{0,1:T(8,128)}, u32[]{:S(2)}) copy-start(f32[512,32]{0,1:T(8,128)} %param.19) | copy-start | bytes 196612
  560.0 80.9 %all-gather.5.cloned.1.call-start = ((), (), s32[]{:S(2)}) async-start(), calls=%async_computation.7 | async-start | bytes 2949120 | tf_op jit(solution)/shard_map/all_gather | solution.py:61
  560.1 45.5 %copy-start.10 = (bf16[512,320]{0,1:T(8,128)(2,1)S(1)}, bf16[512,320]{0,1:T(8,128)(2,1)}, u32[]{:S(2)}) copy-start(bf16[512,320]{0,1:T(8,128)(2,1)} %reduce-scatter.8.cloned.1.call-done) | copy-start | bytes 983044
  607.4 154.9 %reduce-scatter.6.cloned.1.call-start = ((), (), s32[]{:S(2)}) async-start(), calls=%async_computation.5 | async-start | bytes 9437184 | tf_op jit(solution)/shard_map/reduce_scatter | solution.py:37
  644.1 118.2 %copy-start.6 = (bf16[1,128,4096]{2,1,0:T(8,128)(2,1)S(1)}, bf16[1,128,4096]{2,1,0:T(8,128)(2,1)}, u32[]{:S(2)}) copy-start(bf16[1,128,4096]{2,1,0:T(8,128)(2,1)} %param.11) | copy-start | bytes 3145732
  644.1 118.2 %copy-start.19 = (f32[4096]{0:T(1024)S(1)}, f32[4096]{0:T(1024)}, u32[]{:S(2)}) copy-start(f32[4096]{0:T(1024)} %param.13) | copy-start | bytes 49156
  644.1 118.2 %copy-start.23 = (f32[128]{0:T(128)S(1)}, f32[128]{0:T(128)}, u32[]{:S(2)}) copy-start(f32[128]{0:T(128)} %copy-done.22) | copy-start | bytes 1540
  (28 other events, 89.9 us)
Sparse Core Ops, SparseCore 0:
  12.3 112.7 all-gather.2
  489.4 37.3 reduce-scatter.7
  560.1 26.7 reduce-scatter.3
  607.5 33.3 all-gather.4
  645.1 117.1 reduce-scatter.5
where the time goes:
time: 781 us; the launch traced here: 772 us
  matrix products  299 us (38%)
  waiting for transfers between devices  256 us (33%)
  local copies, waits for them, and re-layouts  105 us (13%)
  other arithmetic  47.3 us (6%)
  blocking collectives  36.1 us (5%)
  between operations  17.2 us (2%)
  loops' own time  8.27 us (1%)
    reduce_scatter x1, waiting for transfers between devices, summed_rows(): return lax.psum_scatter(pieces, chips, scatter_dimension=0, tiled=True)[0]  112 us
    all_gather x1, waiting for transfers between devices, per_device(): normed_all = lax.all_gather(normed, TENSOR, axis=0, tiled=True)  111 us
    dot_general x4, matrix products, attend(): jnp.einsum('hst,shd->td', grad_low, query_rows, preferred_element_type=jn...  77.6 us
    dot_general x3, matrix products, product(): jnp.einsum('sc,dc->sd', grad, weight, preferred_element_type=jnp.float32)  55.7 us
    dot_general x4, matrix products, attend(): jnp.einsum('hst,td->shd', grad_low, key_head, preferred_element_type=jnp....  51.1 us
    dynamic_update_slice x12, local copies, waits for them, and re-layouts, per_device(): lax.scan(attend, (empty, empty), starts)  49.8 us
    psum x5, blocking collectives, one_axis_at_a_time(): shard = lax.psum(shard, axis)  36.1 us
    sub x4, matrix products, attend(): attention = jax.nn.softmax(jnp.where(causal[None], scores, -1e+30), axis=2)  32 us
  transfers between devices with their start and end apart: 9, of which 5 were waited for; matrix products, arithmetic and copies ran while one was open for 17% of the time, Pallas kernels for 0%

commit v1 on v0

--- a/solution.py
+++ b/solution.py
@@ -87,7 +87,9 @@
     reciprocal = lax.rsqrt(jnp.mean(inputs * inputs, axis=1, keepdims=True) + norm_eps)
     unit_rows = inputs * reciprocal
     normed = (unit_rows * gain).astype(jnp.bfloat16)
-    normed_all = lax.all_gather(normed, TENSOR, axis=0, tiled=True)
+    normed_all = jnp.concatenate(
+        lax.all_to_all(jnp.stack([normed] * lax.axis_size(TENSOR)), TENSOR, 0, 0), axis=0
+    )
     length = normed_all.shape[0]
     query = rotate(
         jnp.dot(normed_all, w_query, preferred_element_type=jnp.float32) * in_scale,

time: 781 us -> 959 us (1.23)
  waiting for transfers between devices: 256 us -> 397 us
  matrix products: 299 us -> 335 us
  local copies, waits for them, and re-layouts: 105 us -> 78.9 us
  starting transfers between devices: 3.25 us -> 18.8 us
    all_to_all x0 -> x1, waiting for transfers between devices: none -> 251 us  [per_device(): lax.all_to_all(jnp.stack([normed] * lax.axis_size(TENSOR)), TENSOR, 0, 0)]
    all_gather x1 -> x0, waiting for transfers between devices: 111 us -> none  [per_device(): normed_all = lax.all_gather(normed, TENSOR, axis=0, tiled=True)]
    dynamic_update_slice x12 -> x4, local copies, waits for them, and re-layouts: 49.8 us -> 3.9 us  [per_device(): lax.scan(attend, (empty, empty), starts)]
  transfers between devices with their start and end apart: 9 -> 9, of which waited for: 5 -> 4; matrix products, arithmetic and copies ran while one was open for 17% -> 17% of each run, Pallas kernels for 0% -> 0%
where the time goes in v1:
time: 959 us; the launch traced here: 951 us
  waiting for transfers between devices  397 us (41%)
  matrix products  335 us (35%)
  local copies, waits for them, and re-layouts  78.9 us (8%)
  other arithmetic  46.6 us (5%)
  blocking collectives  39.6 us (4%)
  starting transfers between devices  18.8 us (2%)
  between operations  17.4 us (2%)
  loops' own time  17.3 us (2%)
    all_to_all x1, waiting for transfers between devices, per_device(): lax.all_to_all(jnp.stack([normed] * lax.axis_size(TENSOR)), TENSOR, 0, 0)  251 us
    reduce_scatter x1, waiting for transfers between devices, summed_rows(): return lax.psum_scatter(pieces, chips, scatter_dimension=0, tiled=True)[0]  112 us
    dot_general x4, matrix products, attend(): jnp.einsum('hst,shd->td', grad_low, query_rows, preferred_element_type=jn...  77.9 us
    dot_general x3, matrix products, product(): jnp.einsum('sc,dc->sd', grad, weight, preferred_element_type=jnp.float32)  59.6 us
    dot_general x4, matrix products, attend(): jnp.einsum('hst,td->shd', grad_low, key_head, preferred_element_type=jnp....  54.3 us
    psum x5, blocking collectives, one_axis_at_a_time(): shard = lax.psum(shard, axis)  39.6 us
    sub x4, matrix products, attend(): attention = jax.nn.softmax(jnp.where(causal[None], scores, -1e+30), axis=2)  32 us
    all_gather x1, waiting for transfers between devices, in_one_piece(): lax.all_gather(both, axis, axis=dim, tiled=True)  31.7 us
  transfers between devices with their start and end apart: 9, of which 4 were waited for; matrix products, arithmetic and copies ran while one was open for 17% of the time, Pallas kernels for 0%

profile of v1, /device:TPU:1, one launch (start us, length us, event | category | flops | bytes accessed | tf_op | source)
XLA Modules:
  0.0 950.7 jit_solution(13695385576836338748)
XLA Ops:
  16.9 8.6 all-to-all-start
  29.0 250.9 %all-to-all-done = bf16[16,128,4096]{2,1,0:T(8,128)(2,1)} async-done(((bf16[16,128,4096]{2,1,0:T(8,128)(2,1)}), bf16[16,128,4096]{2,1,0:T(8,128)(2,1)}, u32[]{:S(2)}, u32[]{:S(2)}) %all-to-all-start) | async-done | bytes 16777248 | tf_op jit(solution)/shard_map/all_to_all | solution.py:91
  279.9 10.8 %convolution_multiply_fusion.5 = f32[2048,32]{0,1:T(8,128)S(1)} fusion(bf16[2048,4096]{1,0:T(8,128)(2,1)} %bitcast.2, bf16[4096,32]{0,1:T(8,128)(2,1)S(1)} %copy-done.12), kind=kOutput, calls=%fused_computation.78 | convolution fusion | flops 536936448 | bytes 17301504 | tf_op jit(solution)/shard_map/dot_general | solution.py:101
  290.9 10.8 %fusion.72 = bf16[1,2048,32]{1,2,0:T(8,128)(2,1)S(1)} fusion(bf16[2048,4096]{1,0:T(8,128)(2,1)} %bitcast.2, bf16[4096,32]{0,1:T(8,128)(2,1)S(1)} %copy-done.14), kind=kOutput, calls=%fused_computation.80 | convolution fusion | flops 537001984 | bytes 17170432 | tf_op jit(solution)/shard_map/dot_general | solution.py:107
  304.2 9.8 %convolution_multiply_fusion.3 = f32[2048,256]{0,1:T(8,128)} fusion(bf16[2048,4096]{1,0:T(8,128)(2,1)} %bitcast.2, bf16[4096,256]{1,0:T(8,128)(2,1)S(1)} %copy-done), kind=kOutput, calls=%fused_computation.67 | convolution fusion | flops 4295491584 | bytes 20971520 | tf_op jit(solution)/shard_map/dot_general | solution.py:95
  323.3 10.3 %fusion.89 = bf16[2048,256]{0,1:T(8,128)(2,1)} fusion(f32[2048,1]{0,1:T(1,128)S(1)} %get-tuple-element.180, f32[2048,255]{0,1:T(8,128)S(1)} %get-tuple-element.182, f32[2048,255]{0,1:T(8,128)S(1)} %get-tuple-element.181, f32[2048,1]{0,1:T(1,128)S(1)} %get-tuple-element.179, f32[2048,256]{0,1:T(8,128)S(1)} %copy-done.2, f32[256]{0:T(256)S(1)} %multiply_power_fusion.1, ...), kind=kLoop, calls=%fused_computation.98 | loop fusion | flops 4718592 | bytes 7341312 | tf_op jit(solution)/shard_map/convert_element_type | solution.py:99
  338.0 247.3 %while.17 = (s32[]{:T(128)}, f32[2048,128]{1,0:T(8,128)}, f32[2048,128]{1,0:T(8,128)}, bf16[4,512,2,128]{3,2,1,0:T(2,128)(2,1)}, f32[4,512,2,128]{3,1,2,0:T(8,12...) while((s32[]{:T(128)}, f32[2048,128]{1,0:T(8,128)}, ...), condition=%wide.region_5.6_spmd.clone, body=%wide.region_1.5_spmd.clone.sunk | while | flops 3269599744 | bytes 153387344 | solution.py:159
  341.4 8.0 fusion.200
  363.2 19.4 %fusion.201 = f32[2048,128]{1,0:T(8,128)} fusion(f32[512,2,2048]{2,0,1:T(8,128)} %fusion.199, f32[2048,128]{1,0:T(8,128)} %get-tuple-element.280, pred[]{:T(512)S(6)} %compare.41, bf16[2048,2,128]{0,2,1:T(8,128)(2,1)} %get-tuple-element.298, s32[]{:T(128)S(6)} %select_n.302, f32[2,512,2048]{2,1,0:T(8,128)} %get-tuple-element.264, ...), kind=kOutput, calls=%fused_computation.24.clone.1 | convolution fusion | flops 552078336 | bytes 35921924 | tf_op jit(solution)/shard_map/while/body/eval_jaxpr/hst,shd->td/dot_general | solution.py:150
  382.6 13.6 %fusion.204 = f32[4,512,2,128]{3,1,2,0:T(8,128)} fusion(f32[4,512,2,128]{3,1,2,0:T(8,128)} %get-tuple-element.283, s32[]{:T(128)S(6)} %copy.75, f32[512,2,2048]{2,0,1:T(8,128)} %fusion.199, bf16[2048,128]{1,0:T(8,128)(2,1)S(1)} %copy-done.18, f32[2,512,2048]{2,1,0:T(8,128)} %get-tuple-element.264, f32[2,512]{1,0:T(2,128)S(1)} %get-tuple-element.265), kind=kOutput, calls=%fused_computation.29.clone.1 | convolution fusion | flops 551554048 | bytes 34611204 | tf_op jit(solution)/shard_map/while/body/eval_jaxpr/hst,td->shd/dot_general | solution.py:147
  399.6 8.0 fusion.200
  422.6 19.5 %fusion.201 = f32[2048,128]{1,0:T(8,128)} fusion(f32[512,2,2048]{2,0,1:T(8,128)} %fusion.199, f32[2048,128]{1,0:T(8,128)} %get-tuple-element.280, pred[]{:T(512)S(6)} %compare.41, bf16[2048,2,128]{0,2,1:T(8,128)(2,1)} %get-tuple-element.298, s32[]{:T(128)S(6)} %select_n.302, f32[2,512,2048]{2,1,0:T(8,128)} %get-tuple-element.264, ...), kind=kOutput, calls=%fused_computation.24.clone.1 | convolution fusion | flops 552078336 | bytes 35921924 | tf_op jit(solution)/shard_map/while/body/eval_jaxpr/hst,shd->td/dot_general | solution.py:150
  442.1 13.6 %fusion.204 = f32[4,512,2,128]{3,1,2,0:T(8,128)} fusion(f32[4,512,2,128]{3,1,2,0:T(8,128)} %get-tuple-element.283, s32[]{:T(128)S(6)} %copy.75, f32[512,2,2048]{2,0,1:T(8,128)} %fusion.199, bf16[2048,128]{1,0:T(8,128)(2,1)S(1)} %copy-done.18, f32[2,512,2048]{2,1,0:T(8,128)} %get-tuple-element.264, f32[2,512]{1,0:T(2,128)S(1)} %get-tuple-element.265), kind=kOutput, calls=%fused_computation.29.clone.1 | convolution fusion | flops 551554048 | bytes 34611204 | tf_op jit(solution)/shard_map/while/body/eval_jaxpr/hst,td->shd/dot_general | solution.py:147
  459.2 8.0 fusion.200
  482.2 19.5 %fusion.201 = f32[2048,128]{1,0:T(8,128)} fusion(f32[512,2,2048]{2,0,1:T(8,128)} %fusion.199, f32[2048,128]{1,0:T(8,128)} %get-tuple-element.280, pred[]{:T(512)S(6)} %compare.41, bf16[2048,2,128]{0,2,1:T(8,128)(2,1)} %get-tuple-element.298, s32[]{:T(128)S(6)} %select_n.302, f32[2,512,2048]{2,1,0:T(8,128)} %get-tuple-element.264, ...), kind=kOutput, calls=%fused_computation.24.clone.1 | convolution fusion | flops 552078336 | bytes 35921924 | tf_op jit(solution)/shard_map/while/body/eval_jaxpr/hst,shd->td/dot_general | solution.py:150
  501.7 13.6 %fusion.204 = f32[4,512,2,128]{3,1,2,0:T(8,128)} fusion(f32[4,512,2,128]{3,1,2,0:T(8,128)} %get-tuple-element.283, s32[]{:T(128)S(6)} %copy.75, f32[512,2,2048]{2,0,1:T(8,128)} %fusion.199, bf16[2048,128]{1,0:T(8,128)(2,1)S(1)} %copy-done.18, f32[2,512,2048]{2,1,0:T(8,128)} %get-tuple-element.264, f32[2,512]{1,0:T(2,128)S(1)} %get-tuple-element.265), kind=kOutput, calls=%fused_computation.29.clone.1 | convolution fusion | flops 551554048 | bytes 34611204 | tf_op jit(solution)/shard_map/while/body/eval_jaxpr/hst,td->shd/dot_general | solution.py:147
  518.7 8.0 fusion.200
  541.7 19.5 %fusion.201 = f32[2048,128]{1,0:T(8,128)} fusion(f32[512,2,2048]{2,0,1:T(8,128)} %fusion.199, f32[2048,128]{1,0:T(8,128)} %get-tuple-element.280, pred[]{:T(512)S(6)} %compare.41, bf16[2048,2,128]{0,2,1:T(8,128)(2,1)} %get-tuple-element.298, s32[]{:T(128)S(6)} %select_n.302, f32[2,512,2048]{2,1,0:T(8,128)} %get-tuple-element.264, ...), kind=kOutput, calls=%fused_computation.24.clone.1 | convolution fusion | flops 552078336 | bytes 35921924 | tf_op jit(solution)/shard_map/while/body/eval_jaxpr/hst,shd->td/dot_general | solution.py:150
  561.2 13.6 %fusion.204 = f32[4,512,2,128]{3,1,2,0:T(8,128)} fusion(f32[4,512,2,128]{3,1,2,0:T(8,128)} %get-tuple-element.283, s32[]{:T(128)S(6)} %copy.75, f32[512,2,2048]{2,0,1:T(8,128)} %fusion.199, bf16[2048,128]{1,0:T(8,128)(2,1)S(1)} %copy-done.18, f32[2,512,2048]{2,1,0:T(8,128)} %get-tuple-element.264, f32[2,512]{1,0:T(2,128)S(1)} %get-tuple-element.265), kind=kOutput, calls=%fused_computation.29.clone.1 | convolution fusion | flops 551554048 | bytes 34611204 | tf_op jit(solution)/shard_map/while/body/eval_jaxpr/hst,td->shd/dot_general | solution.py:147
  615.3 9.8 %fusion.83 = bf16[4,512,2,128]{3,1,2,0:T(8,128)(2,1)S(1)} fusion(f32[4,512,2,128]{3,1,2,0:T(8,128)} %get-tuple-element.69, f32[4,512,2,128]{3,1,2,0:T(8,128)} %copy.47, f32[4,512,2,128]{3,1,2,0:T(8,128)} %copy.48, f32[2,128]{1,0:T(2,128)S(1)} %copy-done.33, f32[4,512]{1,0:T(4,128)S(1)} %copy-done.22, pred[2,128]{1,0:T(4,128)(4,1)S(1)} %copy-done.34), kind=kLoop, calls=%fused_computation.91 | loop fusion | flops 3670016 | bytes 7349504 | tf_op jit(solution)/shard_map/convert_element_type | solution.py:177
  628.1 10.6 %fusion.64 = bf16[4096,256]{0,1:T(8,128)(2,1)S(1)} fusion(bf16[2048,4096]{1,0:T(8,128)(2,1)} %bitcast.2, bf16[256,8,2,128]{3,2,1,0:T(2,128)(2,1)S(1)} %bitcast.210), kind=kOutput, calls=%fused_computation.60 | convolution fusion | flops 4297064448 | bytes 19922944 | tf_op jit(solution)/shard_map/sd,sc->dc/dot_general | solution.py:195
  638.9 8.8 fusion.66
  648.4 7.8 fusion.65
  658.9 13.6 %fusion.130 = f32[2048,4096]{1,0:T(8,128)} fusion(bf16[4096,32]{0,1:T(8,128)(2,1)S(1)} %copy-done.15, f32[2,2048,32]{1,2,0:T(8,128)S(1)} %convert_add_fusion.1), kind=kOutput, calls=%fused_computation.168 | convolution fusion | flops 536870912 | bytes 33947648 | tf_op jit(solution)/shard_map/sc,dc->sd/dot_general | solution.py:180
  672.5 13.9 %fusion.114 = f32[2048,4096]{1,0:T(8,128)} fusion(bf16[4096,32]{0,1:T(8,128)(2,1)S(1)} %copy-done.13, f32[2048,1]{0,1:T(1,128)S(1)} %get-tuple-element.189, f32[2048,31]{0,1:T(8,128)S(1)} %copy-done.16, f32[2048,31]{0,1:T(8,128)S(1)} %get-tuple-element.193, f32[2048,1]{0,1:T(1,128)S(1)} %get-tuple-element.188, f32[32]{0:T(128)S(1)} %copy-done.26, ...), kind=kOutput, calls=%fused_computation.149 | convolution fusion | flops 537526272 | bytes 34620416 | tf_op jit(solution)/shard_map/sc,dc->sd/dot_general | solution.py:180
  686.4 32.2 %multiply_convert_fusion = bf16[2048,4096]{1,0:T(8,128)(2,1)} fusion(f32[2048,4096]{1,0:T(8,128)} %fusion.130, f32[2048,4096]{1,0:T(8,128)} %fusion.114, bf16[4096,256]{1,0:T(8,128)(2,1)S(1)} %copy-done, f32[2048,256]{0,1:T(8,128)} %get-tuple-element.199, f32[2048,256]{0,1:T(8,128)} %get-tuple-element.200, f32[2048,256]{0,1:T(8,128)} %bitcast.205, ...), kind=kOutput, calls=%fused_computation.58 | convolution fusion | flops 4332191744 | bytes 92275968 | tf_op jit(solution)/shard_map/sc,dc->sd/dot_general | solution.py:180
  718.5 14.0 %copy.44 = bf16[2,8,128,4096]{3,2,1,0:T(8,128)(2,1)} copy(bf16[2,8,128,4096]{3,2,0,1:T(8,128)(2,1)} %bitcast.201) | data formatting | bytes 33554432 | tf_op jit(solution)/shard_map/transpose | solution.py:35
  742.0 10.3 %psum.36 = f32[]{:T(128)} all-reduce(f32[]{:T(128)} %psum.35), channel_id=1, replica_groups=mesh['dp_0'=2,'dp_1'=4,'tensor_0'=2,'tensor_1'=4,'tensor_2'=2] {'dp_1'}, use_global_device_ids=true, to_apply=%region_14.15 | all-reduce | flops 1 | bytes 8 | tf_op jit(solution)/shard_map/psum | solution.py:51
  759.1 10.2 %psum.38 = f32[]{:T(128)} all-reduce(f32[]{:T(128)} %psum.37), channel_id=1, replica_groups=mesh['dp_0'=2,'dp_1'=4,'tensor_0'=2,'tensor_1'=4,'tensor_2'=2] {'tensor_1'}, use_global_device_ids=true, to_apply=%region_16.17 | all-reduce | flops 1 | bytes 8 | tf_op jit(solution)/shard_map/psum | solution.py:51
  770.5 8.9 psum.39
  787.6 31.7 %all-gather.2.cloned.1.call-done = bf16[4096,320]{0,1:T(8,128)(2,1)} async-done(((bf16[512,320]{0,1:T(8,128)(2,1)}), bf16[4096,320]{0,1:T(8,128)(2,1)}) %all-gather.2.cloned.1.call-update) | async-done | bytes 2621456 | tf_op jit(solution)/shard_map/all_gather | solution.py:61
  828.5 111.8 %reduce-scatter.6.cloned.1.call-done = bf16[1,128,4096]{2,1,0:T(8,128)(2,1)} async-done(((bf16[8,128,4096]{2,1,0:T(8,128)(2,1)}), bf16[1,128,4096]{2,1,0:T(8,128)(2,1)}) %reduce-scatter.6.cloned.1.call-update) | async-done | bytes 1048592 | tf_op jit(solution)/shard_map/reduce_scatter | solution.py:37
  (210 shorter events, 167.1 us)
Async XLA Ops:
  7.2 297.1 %copy-start = (bf16[4096,256]{1,0:T(8,128)(2,1)S(1)}, bf16[4096,256]{1,0:T(8,128)(2,1)}, u32[]{:S(2)}) copy-start(bf16[4096,256]{1,0:T(8,128)(2,1)} %param.14) | copy-start | bytes 6291460
  16.9 263.0 %all-to-all-start = ((bf16[16,128,4096]{2,1,0:T(8,128)(2,1)}), bf16[16,128,4096]{2,1,0:T(8,128)(2,1)}, u32[]{:S(2)}, u32[]{:S(2)}) async-start(bf16[16,128,4096]{2,1,0:T(8,128)(2,1)} %stack.20), calls=%async_computation | async-start | bytes 33554432 | tf_op jit(solution)/shard_map/all_to_all | solution.py:91
  25.5 254.4 %copy-start.12 = (bf16[4096,32]{0,1:T(8,128)(2,1)S(1)}, bf16[4096,32]{0,1:T(8,128)(2,1)}, u32[]{:S(2)}) copy-start(bf16[4096,32]{0,1:T(8,128)(2,1)} %param.15) | copy-start | bytes 786436
  25.5 707.1 %reduce-scatter.8.cloned.1.call-start = ((), (), s32[]{:S(2)}) async-start(), calls=%async_computation.6 | async-start | bytes 2949120 | tf_op jit(solution)/shard_map/reduce_scatter | solution.py:42
  27.1 274.5 %copy-start.23 = (pred[32]{0:T(512)(128)(4,1)}, pred[32]{0:T(512)(128)(4,1)S(1)}, u32[]{:S(2)}) copy-start(pred[32]{0:T(512)(128)(4,1)S(1)} %fusion.136) | copy-start | bytes 100
  27.2 274.5 %copy-start.25 = (f32[32]{0:T(128)}, f32[32]{0:T(128)S(1)}, u32[]{:S(2)}) copy-start(f32[32]{0:T(128)S(1)} %multiply_power_fusion.2) | copy-start | bytes 388
  27.2 296.1 %copy-start.29 = (pred[256]{0:T(512)(128)(4,1)}, pred[256]{0:T(512)(128)(4,1)S(1)}, u32[]{:S(2)}) copy-start(pred[256]{0:T(512)(128)(4,1)S(1)} %fusion.133) | copy-start | bytes 772
  27.8 295.5 %copy-start.27 = (f32[256]{0:T(256)}, f32[256]{0:T(256)S(1)}, u32[]{:S(2)}) copy-start(f32[256]{0:T(256)S(1)} %multiply_power_fusion.1) | copy-start | bytes 3076
  279.9 10.9 %copy-start.14 = (bf16[4096,32]{0,1:T(8,128)(2,1)S(1)}, bf16[4096,32]{0,1:T(8,128)(2,1)}, u32[]{:S(2)}) copy-start(bf16[4096,32]{0,1:T(8,128)(2,1)} %param.16) | copy-start | bytes 786436
  303.1 13.8 %collective-permute-start = (bf16[2,2048,32]{1,2,0:T(8,128)(2,1)S(1)}, bf16[2,2048,32]{1,2,0:T(8,128)(2,1)S(1)}, u32[]{:S(2)}, u32[]{:S(2)}) collective-permute-start(bf16[2,2048,32]{1,2,0:T(8,128)(2,1)S(1)} %pad_maximum_fusion.4), channel_id=1, source_target_pairs={{0,1},{1,0},{2,3},{3,2},{4,5},{5,4},{6,7},{7,6},{8,9},{9,8},{10,11... | collective-permute-start | bytes 786440 | tf_op jit(solution)/shard_map/ppermute | solution.py:22
  317.0 18.6 %collective-permute-start.1 = (bf16[2,2048,64]{1,2,0:T(8,128)(2,1)S(1)}, bf16[2,2048,64]{1,2,0:T(8,128)(2,1)S(1)}, u32[]{:S(2)}, u32[]{:S(2)}) collective-permute-start(bf16[2,2048,64]{1,2,0:T(8,128)(2,1)S(1)} %maximum_select_fusion.1), channel_id=1, source_target_pairs={{0,2},{1,3},{2,0},{3,1},{4,6},{5,7},{6,4},{7,5},{8,10},{9,11},{10,... | collective-permute-start | bytes 1572872 | tf_op jit(solution)/shard_map/ppermute | solution.py:22
  363.2 19.4 %copy-start.18 = (bf16[2048,128]{1,0:T(8,128)(2,1)S(1)}, bf16[2048,128]{1,0:T(8,128)(2,1)}, u32[]{:S(2)}) copy-start(bf16[2048,128]{1,0:T(8,128)(2,1)} %get-tuple-element.299) | copy-start | bytes 1572868 | tf_op jit(solution)/shard_map/while
  422.6 19.5 %copy-start.18 = (bf16[2048,128]{1,0:T(8,128)(2,1)S(1)}, bf16[2048,128]{1,0:T(8,128)(2,1)}, u32[]{:S(2)}) copy-start(bf16[2048,128]{1,0:T(8,128)(2,1)} %get-tuple-element.299) | copy-start | bytes 1572868 | tf_op jit(solution)/shard_map/while
  482.2 19.5 %copy-start.18 = (bf16[2048,128]{1,0:T(8,128)(2,1)S(1)}, bf16[2048,128]{1,0:T(8,128)(2,1)}, u32[]{:S(2)}) copy-start(bf16[2048,128]{1,0:T(8,128)(2,1)} %get-tuple-element.299) | copy-start | bytes 1572868 | tf_op jit(solution)/shard_map/while
  541.7 19.5 %copy-start.18 = (bf16[2048,128]{1,0:T(8,128)(2,1)S(1)}, bf16[2048,128]{1,0:T(8,128)(2,1)}, u32[]{:S(2)}) copy-start(bf16[2048,128]{1,0:T(8,128)(2,1)} %get-tuple-element.299) | copy-start | bytes 1572868 | tf_op jit(solution)/shard_map/while
  598.1 28.0 %collective-permute-start.2 = (bf16[2,2048,64]{1,2,0:T(8,128)(2,1)S(1)}, bf16[2,2048,64]{1,2,0:T(8,128)(2,1)S(1)}, u32[]{:S(2)}, u32[]{:S(2)}) collective-permute-start(bf16[2,2048,64]{1,2,0:T(8,128)(2,1)S(1)} %select_convert_fusion), channel_id=1, source_target_pairs={{0,2},{1,3},{2,0},{3,1},{4,6},{5,7},{6,4},{7,5},{8,10},{9,11},{10,... | collective-permute-start | bytes 1572872 | tf_op jit(solution)/shard_map/ppermute | solution.py:22
  626.9 11.8 %collective-permute-start.3 = (bf16[2,2048,32]{1,2,0:T(8,128)(2,1)S(1)}, bf16[2,2048,32]{1,2,0:T(8,128)(2,1)S(1)}, u32[]{:S(2)}, u32[]{:S(2)}) collective-permute-start(bf16[2,2048,32]{1,2,0:T(8,128)(2,1)S(1)} %select_convert_fusion.1), channel_id=1, source_target_pairs={{0,1},{1,0},{2,3},{3,2},{4,5},{5,4},{6,7},{7,6},{8,9},{9,8},{10,11... | collective-permute-start | bytes 786440 | tf_op jit(solution)/shard_map/ppermute | solution.py:22
  638.8 9.6 %copy-start.24 = (pred[32]{0:T(512)(128)(4,1)S(1)}, pred[32]{0:T(512)(128)(4,1)}, u32[]{:S(2)}) copy-start(pred[32]{0:T(512)(128)(4,1)} %copy-done.23) | copy-start | bytes 100
  638.9 9.6 %copy-start.26 = (f32[32]{0:T(128)S(1)}, f32[32]{0:T(128)}, u32[]{:S(2)}) copy-start(f32[32]{0:T(128)} %copy-done.25) | copy-start | bytes 388
  658.0 14.5 %copy-start.13 = (bf16[4096,32]{0,1:T(8,128)(2,1)S(1)}, bf16[4096,32]{0,1:T(8,128)(2,1)}, u32[]{:S(2)}) copy-start(bf16[4096,32]{0,1:T(8,128)(2,1)} %param.15) | copy-start | bytes 786436
  658.0 125.6 %reduce-scatter.4.cloned.1.call-start = ((), (), s32[]{:S(2)}) async-start(), calls=%async_computation.4 | async-start | bytes 25165824 | tf_op jit(solution)/shard_map/reduce_scatter | solution.py:36
  658.9 13.6 %copy-start.16 = (f32[2048,31]{0,1:T(8,128)S(1)}, f32[2048,31]{0,1:T(8,128)}, u32[]{:S(2)}) copy-start(f32[2048,31]{0,1:T(8,128)} %get-tuple-element.194) | copy-start | bytes 761860
  672.5 13.9 %copy-start.28 = (f32[256]{0:T(256)S(1)}, f32[256]{0:T(256)}, u32[]{:S(2)}) copy-start(f32[256]{0:T(256)} %copy-done.27) | copy-start | bytes 3076
  672.5 13.9 %copy-start.30 = (pred[256]{0:T(512)(128)(4,1)S(1)}, pred[256]{0:T(512)(128)(4,1)}, u32[]{:S(2)}) copy-start(pred[256]{0:T(512)(128)(4,1)} %copy-done.29) | copy-start | bytes 772
  732.5 47.6 %copy-start.20 = (f32[512,32]{0,1:T(8,128)S(1)}, f32[512,32]{0,1:T(8,128)}, u32[]{:S(2)}) copy-start(f32[512,32]{0,1:T(8,128)} %param.18) | copy-start | bytes 196612
  732.6 47.6 %copy-start.21 = (f32[512,32]{0,1:T(8,128)S(1)}, f32[512,32]{0,1:T(8,128)}, u32[]{:S(2)}) copy-start(f32[512,32]{0,1:T(8,128)} %param.19) | copy-start | bytes 196612
  732.6 86.8 %all-gather.2.cloned.1.call-start = ((), (), s32[]{:S(2)}) async-start(), calls=%async_computation.7 | async-start | bytes 2949120 | tf_op jit(solution)/shard_map/all_gather | solution.py:61
  732.7 47.5 %copy-start.11 = (bf16[512,320]{0,1:T(8,128)(2,1)S(1)}, bf16[512,320]{0,1:T(8,128)(2,1)}, u32[]{:S(2)}) copy-start(bf16[512,320]{0,1:T(8,128)(2,1)} %reduce-scatter.8.cloned.1.call-done) | copy-start | bytes 983044
  783.5 156.8 %reduce-scatter.6.cloned.1.call-start = ((), (), s32[]{:S(2)}) async-start(), calls=%async_computation.5 | async-start | bytes 9437184 | tf_op jit(solution)/shard_map/reduce_scatter | solution.py:37
  822.5 117.8 %copy-start.4 = (bf16[1,128,4096]{2,1,0:T(8,128)(2,1)S(1)}, bf16[1,128,4096]{2,1,0:T(8,128)(2,1)}, u32[]{:S(2)}) copy-start(bf16[1,128,4096]{2,1,0:T(8,128)(2,1)} %param.11) | copy-start | bytes 3145732
  822.5 117.8 %copy-start.19 = (f32[4096]{0:T(1024)S(1)}, f32[4096]{0:T(1024)}, u32[]{:S(2)}) copy-start(f32[4096]{0:T(1024)} %param.13) | copy-start | bytes 49156
  822.5 117.8 %copy-start.32 = (f32[128]{0:T(128)S(1)}, f32[128]{0:T(128)}, u32[]{:S(2)}) copy-start(f32[128]{0:T(128)} %copy-done.31) | copy-start | bytes 1540
  (25 other events, 98.6 us)
Sparse Core Ops, SparseCore 0:
  658.1 42.9 reduce-scatter.7
  732.7 32.2 reduce-scatter.3
  783.7 35.6 all-gather.1
  823.5 116.7 reduce-scatter.5
